TPU v7x, 32 devices: a whole 2x2x4 slice. The times are simulated.
32 devices in a mesh: mol: 2 (over y), pair: 4 (over z), virt: 2 (over x), rep: 2 (over core).
Axes of the slice: x: 2, y: 2, z: 4, core: 2. Of those that a mesh axis runs over, the one named last changes fastest.
Arguments:
- amplitudes: bfloat16 [12, 32, 384, 384], P(('mol', 'rep'), None, 'pair', 'virt'), parts along dimension 0, may hold values from -6 to 6
- integrals: bfloat16 [64, 384, 32, 384], P('mol', 'virt', 'pair'), parts along dimension 0, may hold values from -0.15625 to 0.15625
- occ_irrep: int32 [32], replicated, may hold values from 0 to 7, as said below
- virt_irrep: int32 [384], replicated, may hold values from 0 to 7, as said below
Outputs:
- cycle_term: float32 [384, 12, 32, 384], P('virt', ('mol', 'rep'), 'pair'), parts along dimension 1
There are 2 independent parts, one for each index of `mol`. A program takes and returns all parts, laid end to end along the dimension named above; an argument that names none is the same for every part. Nothing has to cross between parts.
Inputs may be any that keep to these rules, and one draw needn't show every extreme that they name: `occ_irrep`: labels never fall along the orbitals, the first is 0 and the last is 7. `virt_irrep`: labels never fall along the orbitals, the first is 0 and the last is 7.
All inputs are finite; a program needn't handle non-finite values.
Results may differ from a plain program's by a relative error of at most 0.0003.
Values may be sent and summed in bfloat16 or wider, within the bound.
A program may use at most 192 MiB of HBM per device.

v0:
```python
import jax
import jax.numpy as jnp
from jax import lax
from jax.sharding import PartitionSpec as P


def shards(amplitudes, integrals, occ_irrep, virt_irrep):
    occ_local = amplitudes.shape[0]
    virt_pair = amplitudes.shape[2]
    virt_slice = amplitudes.shape[3]
    occ_pair = integrals.shape[2]
    sym_i = lax.dynamic_slice_in_dim(occ_irrep, lax.axis_index("rep") * occ_local, occ_local)
    sym_a = lax.dynamic_slice_in_dim(virt_irrep, lax.axis_index("pair") * virt_pair, virt_pair)
    sym_c = lax.dynamic_slice_in_dim(virt_irrep, lax.axis_index("virt") * virt_slice, virt_slice)
    sym_j = lax.dynamic_slice_in_dim(occ_irrep, lax.axis_index("pair") * occ_pair, occ_pair)
    sym_amps = (
        sym_i[:, None, None, None]
        ^ occ_irrep[None, :, None, None]
        ^ sym_a[None, None, :, None]
        ^ sym_c[None, None, None, :]
    )
    masked_amps = jnp.where(sym_amps == 0, amplitudes, jnp.zeros_like(amplitudes))
    result_mask = None
    result_mask = (
        sym_i[None, :, None, None] ^ sym_j[None, None, :, None] ^ virt_irrep[None, None, None, :]
    )
    partial_value = jnp.einsum(
        "ikac,kcjb->aijb",
        lax.all_gather(masked_amps, "pair", axis=2, tiled=True),
        integrals,
        preferred_element_type=jnp.float32,
    )
    cycle_local = lax.psum_scatter(partial_value, "virt", scatter_dimension=0, tiled=True)
    virt_rows = lax.dynamic_slice_in_dim(
        virt_irrep, lax.axis_index("virt") * cycle_local.shape[0], cycle_local.shape[0]
    )
    full_mask = virt_rows[:, None, None, None] ^ result_mask
    cycle_local = jnp.where(full_mask == 0, cycle_local, jnp.zeros_like(cycle_local))
    return cycle_local


def solution(mesh):
    return jax.shard_map(
        shards,
        mesh=mesh,
        in_specs=(
            P(("mol", "rep"), None, "pair", "virt"),
            P("mol", "virt", "pair", None),
            P(),
            P(),
        ),
        out_specs=P("virt", ("mol", "rep"), "pair", None),
        check_vma=False,
    )
```

profile of v0, /device:TPU:0, one launch (start us, length us, event | category | flops | bytes accessed | tf_op | source)
XLA Modules:
  0.0 581.5 jit_solution(18014122870905853969)
XLA Ops:
  6.5 0.0 all-gather.2.cloned.1.call-start
  6.5 0.7 dynamic_slice.14
  7.3 0.7 broadcast_xor_fusion.2
  8.0 0.8 dynamic_slice.16
  8.7 0.8 dynamic_slice.13
  9.5 0.1 broadcast_xor_fusion
  9.6 5.8 fusion.4
  15.4 0.0 all-gather.2.cloned.1.call-update
  15.4 0.0 reduce-scatter.2.cloned.1.call-start
  15.5 325.4 %all-gather.2.cloned.1.call-done = bf16[3,32,384,192]{3,2,1,0:T(8,128)(2,1)} async-done(((bf16[3,32,96,192]{3,2,1,0:T(8,128)(2,1)}), bf16[3,32,384,192]{3,2,1,0:T(8,128)(2,1)}) %all-gather.2.cloned.1.call-update) | async-done | bytes 14155792 | tf_op jit(solution)/shard_map/all_gather | solution.py:29
  340.8 62.1 %fusion.6 = f32[384,3,8,384]{3,0,2,1:T(8,128)} fusion(bf16[32,192,8,384]{3,2,1,0:T(8,128)(2,1)} %param.5, bf16[3,32,384,192]{3,2,1,0:T(8,128)(2,1)} %all-gather.2.cloned.1.call-done), kind=kOutput, calls=%fused_computation.8 | convolution fusion | flops 43486543872 | bytes 66060288 | tf_op jit(solution)/shard_map/ikac,kcjb->aijb/dot_general | solution.py:27
  402.9 0.0 copy-start.1
  402.9 0.0 copy-start
  402.9 0.0 reduce-scatter.2.cloned.1.call-update
  402.9 0.6 copy-done.1
  403.6 0.1 dynamic_slice.15
  403.6 0.1 broadcast_xor_fusion.3
  403.7 0.0 copy-done
  403.7 0.1 broadcast_xor_fusion.1
  403.8 159.6 %reduce-scatter.2.cloned.1.call-done = f32[192,3,8,384]{3,0,2,1:T(8,128)} async-done(((f32[384,3,8,384]{3,0,2,1:T(8,128)}), f32[192,3,8,384]{3,0,2,1:T(8,128)}) %reduce-scatter.2.cloned.1.call-update) | async-done | bytes 7077904 | tf_op jit(solution)/shard_map/reduce_scatter | solution.py:33
  563.4 4.3 fusion.5
  567.6 7.1 %copy.6 = f32[192,3,8,384]{3,2,1,0:T(8,128)} copy(f32[192,3,8,384]{3,0,2,1:T(8,128)S(1)} %fusion.5) | data formatting | bytes 14155776 | tf_op jit(solution)/shard_map/jit(_where)/select_n | solution.py:38
Async XLA Ops:
  6.5 334.3 %all-gather.2.cloned.1.call-start = ((), (), s32[]{:S(2)}) async-start(), calls=%async_computation.1 | async-start | bytes 23592960 | tf_op jit(solution)/shard_map/all_gather | solution.py:29
  15.4 548.0 %reduce-scatter.2.cloned.1.call-start = ((), (), s32[]{:S(2)}) async-start(), calls=%async_computation.2 | async-start | bytes 21233664 | tf_op jit(solution)/shard_map/reduce_scatter | solution.py:33
  402.9 0.7 copy-start.1
  402.9 0.8 copy-start
Sparse Core Ops, SparseCore 0:
  15.5 325.2 all-gather.1
  403.1 160.2 reduce-scatter.1
where the time goes:
time: 582 us
  waiting for transfers between devices  485 us (83%)
  matrix products  62.1 us (11%)
  between operations  13.4 us (2%)
  other arithmetic  11 us (2%)
  local copies, waits for them, and re-layouts  10 us (2%)
    all_gather x1, waiting for transfers between devices, shards(): lax.all_gather(masked_amps, 'pair', axis=2, tiled=True)  325 us
    reduce_scatter x1, waiting for transfers between devices, shards(): lax.psum_scatter(partial_value, 'virt', scatter_dimension=0, tiled=True)  160 us
    dot_general x1, matrix products, shards(): jnp.einsum('ikac,kcjb->aijb', lax.all_gather(masked_amps, 'pair', axis=2,...  62.1 us
  transfers between devices with their start and end apart: 2, of which 2 were waited for; matrix products, arithmetic and copies ran while one was open for 0% of the time, Pallas kernels for 0%

commit v1 on v0

v1 whole, which is shorter than its diff:
```python
import functools

import jax
import jax.numpy as jnp
from jax import lax
from jax.experimental import pallas as pl
from jax.experimental.pallas import tpu as pltpu
from jax.sharding import PartitionSpec as P

LANES = 128
VMEM_LIMIT = 56 * 1024 * 1024


def dense(amplitudes, integrals, sym_i, sym_a, sym_c, sym_j, occ_irrep, virt_irrep):
    sym_amps = (
        sym_i[:, None, None, None]
        ^ occ_irrep[None, :, None, None]
        ^ sym_a[None, None, :, None]
        ^ sym_c[None, None, None, :]
    )
    masked_amps = jnp.where(sym_amps == 0, amplitudes, jnp.zeros_like(amplitudes))
    partial_value = jnp.einsum(
        "ikac,kcjb->aijb",
        lax.all_gather(masked_amps, "pair", axis=2, tiled=True),
        integrals,
        preferred_element_type=jnp.float32,
    )
    cycle_local = lax.psum_scatter(partial_value, "virt", scatter_dimension=0, tiled=True)
    virt_rows = lax.dynamic_slice_in_dim(
        virt_irrep, lax.axis_index("virt") * cycle_local.shape[0], cycle_local.shape[0]
    )
    full_mask = (
        virt_rows[:, None, None, None]
        ^ sym_i[None, :, None, None]
        ^ sym_j[None, None, :, None]
        ^ virt_irrep[None, None, None, :]
    )
    return jnp.where(full_mask == 0, cycle_local, jnp.zeros_like(cycle_local))


def fold_amps_kernel(pack, syms_ref, row_ref, amps_ref, fold_ref, out_ref):
    kks = out_ref.shape[1]
    i = pl.program_id(0)
    labels = row_ref[...]

    @pl.loop(0, kks)
    def _(kk):
        total = None
        for h in range(pack):
            k = kk + h * kks
            keep = labels == syms_ref[i, k]
            block = jnp.where(keep, amps_ref[0, k].astype(jnp.float32), 0.0).astype(jnp.bfloat16)
            term = jnp.dot(block, fold_ref[h], preferred_element_type=jnp.float32)
            total = term if total is None else total + term
        out_ref[0, kk] = total.astype(jnp.bfloat16)


def fold_ints_kernel(pack, occ_ref, table_ref, ints_ref, fold_ref, out_ref, held):
    virts, occs, orbitals = ints_ref.shape[1:]
    label = occ_ref[pl.program_id(0)]
    chunk = 32
    for start in range(0, virts, chunk):
        rows = pl.ds(start, chunk)
        keep = table_ref[rows] == label
        block = jnp.where(keep, ints_ref[0, rows].astype(jnp.float32), 0.0)
        block = block.reshape(chunk * occs, orbitals).astype(jnp.bfloat16)
        held[pl.ds(start * occs, chunk * occs), :] = jnp.dot(
            block, fold_ref[...], preferred_element_type=jnp.float32
        )
    lane = lax.broadcasted_iota(jnp.int32, (virts, LANES), 1)
    for group in range(occs // pack):
        value = held[pl.ds(group * pack, virts, stride=occs), :]
        for h in range(1, pack):
            other = held[pl.ds(group * pack + h, virts, stride=occs), :]
            value = jnp.where(lane < h * (LANES // pack), value, other)
        out_ref[0, 0, :, pl.ds(group * LANES, LANES)] = value.astype(jnp.bfloat16)


def contract_kernel(row_ref, col_ref, amps_ref, unfold_ref, ints_ref, out_ref, block):
    pairs, _, kks, virts, _ = amps_ref.shape
    width = unfold_ref.shape[1]
    for kk in range(kks):
        for p in range(pairs):
            value = jnp.dot(amps_ref[p, 0, kk], unfold_ref[...], preferred_element_type=jnp.float32)
            keep = row_ref[0, pl.ds(p * virts, virts), :] == col_ref[kk]
            block[pl.ds(p * virts, virts), pl.ds(kk * width, width)] = jnp.where(
                keep, value, 0.0
            ).astype(jnp.bfloat16)
    total = jnp.dot(block[...], ints_ref[...], preferred_element_type=jnp.float32)

    @pl.when(pl.program_id(1) == 0)
    def _():
        out_ref[0] = total

    @pl.when(pl.program_id(1) > 0)
    def _():
        out_ref[0] += total


def unfold_kernel(pack, row_ref, col_ref, part_ref, unfold_ref, out_ref):
    occs = out_ref.shape[2]
    for group in range(occs // pack):
        value = part_ref[0, :, pl.ds(group * LANES, LANES)]
        high = value.astype(jnp.bfloat16)
        low = (value - high.astype(jnp.float32)).astype(jnp.bfloat16)
        both = jnp.concatenate([high, low], axis=1)
        for h in range(pack):
            j = group * pack + h
            full = jnp.dot(both, unfold_ref[h], preferred_element_type=jnp.float32)
            out_ref[:, 0, j, :] = jnp.where(row_ref[0] == col_ref[j], full, 0.0)


def params():
    return pltpu.CompilerParams(vmem_limit_bytes=VMEM_LIMIT)


def one_hot(slots, cap, count, dtype=jnp.bfloat16):
    lanes = lax.broadcasted_iota(jnp.int32, (count, 1, LANES), 2)
    shift = lax.broadcasted_iota(jnp.int32, (count, 1, 1), 0) * cap
    return (slots[None, :, None] + shift == lanes).astype(dtype)


def folded(cap, amplitudes, integrals, sym_i, sym_a, sym_c, sym_j, occ_irrep, virt_irrep):
    pack = LANES // cap
    occ_i, occs, virt_a, virt_c = amplitudes.shape
    occ_j, orbitals = integrals.shape[2:]
    kks = occs // pack
    pairs = orbitals // virt_a
    first = jnp.sum((virt_irrep[None, :] < virt_irrep[:, None]).astype(jnp.int32), axis=1)
    slot_b = jnp.arange(orbitals, dtype=jnp.int32) - first
    begin_c = lax.axis_index("virt") * virt_c
    first_c = lax.dynamic_slice_in_dim(first, begin_c, virt_c)
    slot_c = jnp.arange(virt_c, dtype=jnp.int32) + begin_c - jnp.maximum(first_c, begin_c)

    whole = lambda *dims: pl.BlockSpec(dims, lambda *_: (0,) * len(dims))
    smem = pl.BlockSpec(memory_space=pltpu.SMEM)
    fold_c = one_hot(slot_c, cap, pack)
    small = pl.pallas_call(
        functools.partial(fold_amps_kernel, pack),
        grid=(occ_i,),
        in_specs=[
            smem,
            whole(virt_a, virt_c),
            pl.BlockSpec((1, occs, virt_a, virt_c), lambda i: (i, 0, 0, 0)),
            whole(pack, virt_c, LANES),
        ],
        out_specs=pl.BlockSpec((1, kks, virt_a, LANES), lambda i: (i, 0, 0, 0)),
        out_shape=jax.ShapeDtypeStruct((occ_i, kks, virt_a, LANES), jnp.bfloat16),
        compiler_params=params(),
        name="fold_amps",
    )(sym_i[:, None] ^ occ_irrep[None, :], sym_a[:, None] ^ sym_c[None, :], amplitudes, fold_c)
    gathered = lax.all_gather(small, "pair", axis=0)

    fold_b = one_hot(slot_b, cap, pack).sum(0).astype(jnp.bfloat16)
    ints = pl.pallas_call(
        functools.partial(fold_ints_kernel, pack),
        grid=(occs,),
        in_specs=[
            smem,
            whole(virt_c, occ_j, orbitals),
            pl.BlockSpec((1, virt_c, occ_j, orbitals), lambda k: (k, 0, 0, 0)),
            whole(orbitals, LANES),
        ],
        out_specs=pl.BlockSpec((1, 1, virt_c, occ_j * cap), lambda k: (k % kks, k // kks, 0, 0)),
        out_shape=jax.ShapeDtypeStruct((kks, pack, virt_c, occ_j * cap), jnp.bfloat16),
        scratch_shapes=[pltpu.VMEM((virt_c * occ_j, LANES), jnp.float32)],
        compiler_params=params(),
        cost_estimate=pl.CostEstimate(
            flops=2 * integrals.size * 256, bytes_accessed=2 * integrals.size, transcendentals=0
        ),
        name="fold_ints",
    )(
        occ_irrep,
        sym_c[:, None, None] ^ sym_j[None, :, None] ^ virt_irrep[None, None, :],
        integrals,
        fold_b,
    )
    width = pack * virt_c
    ints = ints.reshape(kks * width, occ_j * cap)

    unfold_c = jnp.concatenate([fold_c[h].T for h in range(pack)], axis=1)
    cols = (occ_irrep.reshape(pack, kks).T[:, :, None] ^ sym_c[None, None, :]).reshape(kks, 1, width)
    rows = (sym_i[:, None] ^ virt_irrep[None, :])[:, :, None]
    step = 4 * pack // 2
    step = min(max(step, 2), kks)
    part = pl.pallas_call(
        contract_kernel,
        grid=(occ_i, kks // step),
        in_specs=[
            pl.BlockSpec((1, orbitals, 1), lambda i, s: (i, 0, 0)),
            pl.BlockSpec((step, 1, width), lambda i, s: (s, 0, 0)),
            pl.BlockSpec((pairs, 1, step, virt_a, LANES), lambda i, s: (0, i, s, 0, 0)),
            whole(LANES, width),
            pl.BlockSpec((step * width, occ_j * cap), lambda i, s: (s, 0)),
        ],
        out_specs=pl.BlockSpec((1, orbitals, occ_j * cap), lambda i, s: (i, 0, 0)),
        out_shape=jax.ShapeDtypeStruct((occ_i, orbitals, occ_j * cap), jnp.float32),
        scratch_shapes=[pltpu.VMEM((orbitals, step * width), jnp.bfloat16)],
        compiler_params=params(),
        name="contract",
    )(rows, cols, gathered, unfold_c, ints)

    total = lax.psum_scatter(part, "virt", scatter_dimension=1, tiled=True)
    virt_v = total.shape[1]
    rows_v = lax.dynamic_slice_in_dim(rows, lax.axis_index("virt") * virt_v, virt_v, axis=1)
    cols_b = (sym_j[:, None] ^ virt_irrep[None, :])[:, None, :]
    unfold_b = one_hot(slot_b, cap, pack).transpose(0, 2, 1)
    unfold_b = jnp.concatenate([unfold_b, unfold_b], axis=1)
    return pl.pallas_call(
        functools.partial(unfold_kernel, pack),
        grid=(occ_i,),
        in_specs=[
            pl.BlockSpec((1, virt_v, 1), lambda i: (i, 0, 0)),
            whole(occ_j, 1, orbitals),
            pl.BlockSpec((1, virt_v, occ_j * cap), lambda i: (i, 0, 0)),
            whole(pack, 2 * LANES, orbitals),
        ],
        out_specs=pl.BlockSpec((virt_v, 1, occ_j, orbitals), lambda i: (0, i, 0, 0)),
        out_shape=jax.ShapeDtypeStruct((virt_v, occ_i, occ_j, orbitals), jnp.float32),
        compiler_params=params(),
        name="unfold",
    )(rows_v, cols_b, total, unfold_b)


def shards(amplitudes, integrals, occ_irrep, virt_irrep):
    occ_local, occs, virt_pair, virt_slice = amplitudes.shape
    occ_pair = integrals.shape[2]
    sym_i = lax.dynamic_slice_in_dim(occ_irrep, lax.axis_index("rep") * occ_local, occ_local)
    sym_a = lax.dynamic_slice_in_dim(virt_irrep, lax.axis_index("pair") * virt_pair, virt_pair)
    sym_c = lax.dynamic_slice_in_dim(virt_irrep, lax.axis_index("virt") * virt_slice, virt_slice)
    sym_j = lax.dynamic_slice_in_dim(occ_irrep, lax.axis_index("pair") * occ_pair, occ_pair)
    args = (amplitudes, integrals, sym_i, sym_a, sym_c, sym_j, occ_irrep, virt_irrep)
    fits = (
        occ_pair % 8 == 0
        and virt_pair % 32 == 0
        and virt_slice % 64 == 0
        and occs % 4 == 0
        and virt_irrep.shape[0] % LANES == 0
    )
    if not fits:
        return dense(*args)
    labels = jnp.arange(8, dtype=jnp.int32)
    largest = jnp.max(jnp.sum((virt_irrep[None, :] == labels[:, None]).astype(jnp.int32), axis=1))
    branch = (largest > 64).astype(jnp.int32) + (largest > 128).astype(jnp.int32)
    return lax.switch(
        branch, [functools.partial(folded, 64), functools.partial(folded, 128), dense], *args
    )


def solution(mesh):
    return jax.shard_map(
        shards,
        mesh=mesh,
        in_specs=(
            P(("mol", "rep"), None, "pair", "virt"),
            P("mol", "virt", "pair", None),
            P(),
            P(),
        ),
        out_specs=P("virt", ("mol", "rep"), "pair", None),
        check_vma=False,
    )
```

time: 582 us -> 189 us (0.32)
  waiting for transfers between devices: 485 us -> 83 us
  Pallas kernels: 0 us -> 69.9 us
  matrix products: 62.1 us -> 0 us
    all_gather x1, waiting for transfers between devices: 325 us -> 52.2 us  [folded(): gathered = lax.all_gather(small, 'pair', axis=0)]
    reduce_scatter x1, waiting for transfers between devices: 160 us -> 30.8 us  [folded(): total = lax.psum_scatter(part, 'virt', scatter_dimension=1, tiled=True)]
    pallas_call x0 -> x4, Pallas kernels: none -> 69.9 us  [the longest x1 34.4 us: folded(): pl.pallas_call(functools.partial(fold_ints_kernel, pack), grid=(occs,), i...]
    dot_general x1 -> x0, matrix products: 62.1 us -> none  [shards(): jnp.einsum('ikac,kcjb->aijb', lax.all_gather(masked_amps, 'pair', axis=2,...]
    select_n x2 -> x0, other arithmetic: 10.1 us -> none  [the longest x1 5.81 us: shards(): jnp.where(sym_amps == 0, amplitudes, jnp.zeros_like(amplitudes))]
    select_n x1 -> x0, local copies, waits for them, and re-layouts: 7.06 us -> none  [shards(): jnp.where(full_mask == 0, cycle_local, jnp.zeros_like(cycle_local))]
  transfers between devices with their start and end apart: 2 -> 2, of which waited for: 2 -> 2; matrix products, arithmetic and copies ran while one was open for 0% -> 4% of each run, Pallas kernels for 0% -> 18%
where the time goes in v1:
time: 189 us; the launch traced here: 187 us
  waiting for transfers between devices  83 us (44%)
  Pallas kernels  69.9 us (37%)
  between operations  14.7 us (8%)
  other arithmetic  11.3 us (6%)
  local copies, waits for them, and re-layouts  8.11 us (4%)
    all_gather x1, waiting for transfers between devices, folded(): gathered = lax.all_gather(small, 'pair', axis=0)  52.2 us
    pallas_call x1, Pallas kernels, folded(): pl.pallas_call(functools.partial(fold_ints_kernel, pack), grid=(occs,), i...  34.4 us
    reduce_scatter x1, waiting for transfers between devices, folded(): total = lax.psum_scatter(part, 'virt', scatter_dimension=1, tiled=True)  30.8 us
    pallas_call x1, Pallas kernels, folded(): pl.pallas_call(contract_kernel, grid=(occ_i, kks // step), in_specs=[pl.B...  19.7 us
    pallas_call x1, Pallas kernels, folded(): pl.pallas_call(functools.partial(fold_amps_kernel, pack), grid=(occ_i,),...  10.6 us
    pallas_call x1, Pallas kernels, folded(): pl.pallas_call(functools.partial(unfold_kernel, pack), grid=(occ_i,), in_...  5.23 us
  transfers between devices with their start and end apart: 2, of which 2 were waited for; matrix products, arithmetic and copies ran while one was open for 4% of the time, Pallas kernels for 18%

profile of v1, /device:TPU:0, one launch (start us, length us, event | category | flops | bytes accessed | tf_op | source)
XLA Modules:
  0.0 187.4 jit_solution(6618511947792128634)
XLA Ops:
  6.5 0.8 convert_reduce_fusion.2
  7.3 0.6 reduce_max.9
  9.3 0.7 dynamic_slice.27
  10.0 0.7 dynamic_slice.28
  10.7 0.8 dynamic_slice.29
  11.5 0.8 dynamic_slice.30
  12.2 165.4 %conditional.1 = (f32[192,3,8,384]{3,2,1,0:T(8,128)S(1)}) conditional(s32[]{:T(128)} %clamp.3, (s32[3]{0:T(128)S(1)}, s32[384]{0:T(512)}, s32[8]{0:T(128)S(1)}, s32[32]{0:T(128)}, s32[192]{0:T(256)S(1)}, /*index=5*/s32[96]{0:T(128)S(1)}, bf16[3,32,96,192]{3,2,1,0:T(8,128)(2,1)}, bf16[32,192,8,384]{3,2,1,0:T(8,128)(2,1)}) %tuple.14, ...), branch_computations={%region_2.0_spmd, %region_6.9_spmd, %region_9.11_spmd} | conditional | flops 43497172992 | bytes 224260608 | solution.py:245
  12.3 1.0 convert_reduce_fusion
  13.3 0.1 maximum_subtract_fusion
  13.5 0.7 copy.25.fold_ref
  14.2 1.3 broadcast_xor_fusion.6.syms_ref
  15.5 0.7 broadcast_xor_fusion.3.row_ref
  16.2 10.6 %fold_amps.2 = bf16[3,16,96,128]{3,2,1,0:T(8,128)(2,1)} custom-call(s32[3,32]{1,0:T(4,128)} %broadcast_xor_fusion.6.syms_ref, s32[96,192]{1,0:T(8,128)} %broadcast_xor_fusion.3.row_ref, bf16[3,32,96,192]{3,2,1,0:T(8,128)(2,1)} %get-tuple-element.63.amps_ref, bf16[2,192,128]{2,1,0:T(8,128)(2,1)} %copy.25.fold_ref), custom_call_target="tpu_custom_call" | custom-call | tf_op jit(solution)/shard_map/cond/branch_0_fun/fold_amps/pallas_call | solution.py:138
  26.9 0.1 reshape.574
  27.0 0.1 copy.24
  27.1 0.1 xor.284
  27.3 0.1 xor.286
  27.4 0.7 pad_maximum_fusion.unfold_ref
  28.2 0.8 fusion.2.fold_ref
  29.0 0.6 broadcast_xor_fusion.4.col_ref
  29.6 0.1 broadcast_xor_fusion.2
  29.7 1.0 broadcast_xor_fusion.1.row_ref
  30.7 1.7 broadcast_xor_fusion.table_ref
  32.4 34.4 %fold_ints.2 = bf16[16,2,192,512]{3,2,1,0:T(8,128)(2,1)} custom-call(s32[32]{0:T(128)S(1)} %copy-done.4, s32[192,8,384]{2,1,0:T(8,128)} %broadcast_xor_fusion.table_ref, bf16[32,192,8,384]{3,2,1,0:T(8,128)(2,1)} %get-tuple-element.64.ints_ref, bf16[384,128]{1,0:T(8,128)(2,1)} %fusion.2.fold_ref), custom_call_target="tpu_custom_call" | custom-call | flops 9663676416 | bytes 37748736 | tf_op jit(solution)/shard_map/cond/branch_0_fun/fold_ints/pallas_call | solution.py:155
  66.9 52.2 %all-gather.6.cloned.1.call-done = bf16[12,16,96,128]{3,2,1,0:T(8,128)(2,1)} async-done(((bf16[3,16,96,128]{3,2,1,0:T(8,128)(2,1)}), bf16[12,16,96,128]{3,2,1,0:T(8,128)(2,1)}) %all-gather.6.cloned.1.call-update) | async-done | bytes 4718608 | tf_op jit(solution)/shard_map/cond/branch_0_fun/all_gather | solution.py:152
  119.1 19.7 %contract.2 = f32[3,384,512]{2,1,0:T(8,128)} custom-call(s32[3,384,1]{2,1,0:T(8,128)} %broadcast_xor_fusion.1.row_ref, s32[16,1,384]{2,1,0:T(1,128)} %broadcast_xor_fusion.4.col_ref, bf16[4,3,16,96,128]{4,3,2,1,0:T(8,128)(2,1)} %bitcast.39, bf16[128,384]{1,0:T(8,128)(2,1)} %pad_maximum_fusion.unfold_ref, bf16[6144,512]{1,0:T(8,128)(2,1)} %bitcast.37), custom_call_target="tpu_custom_call" | custom-call | tf_op jit(solution)/shard_map/cond/branch_0_fun/contract/pallas_call | solution.py:186
  139.0 0.9 copy.26.row_ref
  139.9 0.8 add_convert_fusion.unfold_ref
  140.7 0.7 broadcast_xor_fusion.5.col_ref
  141.4 30.8 %reduce-scatter.4.cloned.1.call-done.part_ref = f32[3,192,512]{2,1,0:T(8,128)} async-done(((f32[3,384,512]{2,1,0:T(8,128)}), f32[3,192,512]{2,1,0:T(8,128)}) %reduce-scatter.4.cloned.1.call-update) | async-done | bytes 1179664 | tf_op jit(solution)/shard_map/cond/branch_0_fun/reduce_scatter | solution.py:203
  172.1 5.2 %unfold.2 = f32[192,3,8,384]{3,2,1,0:T(8,128)S(1)} custom-call(s32[3,192,1]{2,1,0:T(8,128)} %copy.26.row_ref, s32[8,1,384]{2,1,0:T(1,128)} %broadcast_xor_fusion.5.col_ref, f32[3,192,512]{2,1,0:T(8,128)} %reduce-scatter.4.cloned.1.call-done.part_ref, bf16[2,256,384]{2,1,0:T(8,128)(2,1)} %add_convert_fusion.unfold_ref), custom_call_target="tpu_custom_call" | custom-call | tf_op jit(solution)/shard_map/cond/branch_0_fun/unfold/pallas_call | solution.py:209
  177.6 3.0 %copy-done = f32[192,3,8,384]{3,2,1,0:T(8,128)} copy-done((f32[192,3,8,384]{3,2,1,0:T(8,128)}, f32[192,3,8,384]{3,2,1,0:T(8,128)S(1)}, u32[]{:S(2)}) %copy-start) | copy-done | bytes 7077912
  (20 shorter events, 0.6 us)
Async XLA Ops:
  12.2 14.6 %copy-start.4 = (s32[32]{0:T(128)S(1)}, s32[32]{0:T(128)}, u32[]{:S(2)}) copy-start(s32[32]{0:T(128)} %get-tuple-element.60.occ_ref) | copy-start | bytes 388 | tf_op jit(solution)/shard_map/cond
  12.2 17.5 %copy-start.1 = (s32[384]{0:T(512)S(1)}, s32[384]{0:T(512)}, u32[]{:S(2)}) copy-start(s32[384]{0:T(512)} %get-tuple-element.58) | copy-start | bytes 4612 | tf_op jit(solution)/shard_map/cond
  12.3 106.9 %all-gather.6.cloned.1.call-start = ((), (), s32[]{:S(2)}) async-start(), calls=%async_computation.4 | async-start | bytes 5898240 | tf_op jit(solution)/shard_map/cond/branch_0_fun/all_gather | solution.py:152
  26.8 145.3 %reduce-scatter.4.cloned.1.call-start = ((), (), s32[]{:S(2)}) async-start(), calls=%async_computation.3 | async-start | bytes 3538944 | tf_op jit(solution)/shard_map/cond/branch_0_fun/reduce_scatter | solution.py:203
  177.6 3.0 %copy-start = (f32[192,3,8,384]{3,2,1,0:T(8,128)}, f32[192,3,8,384]{3,2,1,0:T(8,128)S(1)}, u32[]{:S(2)}) copy-start(f32[192,3,8,384]{3,2,1,0:T(8,128)S(1)} %get-tuple-element.140) | copy-start | bytes 21233668
Sparse Core Ops, SparseCore 0:
  27.0 92.1 all-gather.5
  138.9 33.1 reduce-scatter.3
